TPU v7x, 256 devices: a whole 4x4x8 slice. The times are simulated.
256 devices in a mesh: grp: 16 (over y, x_lo, core), blk: 16 (over x_hi, z).
Axes of the slice: x: 4 (x_hi: 2, x_lo: 2; x = x_hi * 2 + x_lo), y: 4, z: 8, core: 2. Of those that a mesh axis runs over, the one named last changes fastest.
Arguments:
- patches: bfloat16 [2048, 64, 1152], P(('grp', 'blk')), may hold values from -200 to 200
- probe: bfloat16 [1152], replicated, may hold values from -4 to 4
- w_key: bfloat16 [1152, 1152], P('grp'), may hold values from -0.125 to 1.125
- w_value: bfloat16 [1152, 1152], P('grp'), may hold values from -0.1875 to 0.1875
- w_out: bfloat16 [1152, 1152], P('grp'), may hold values from -0.1875 to 0.1875
- texts: bfloat16 [2048, 1152], P(('grp', 'blk')), may hold values from -4 to 4
Outputs:
- grad_image: float32 [2048, 1152], P(('grp', 'blk'))
- grad_text: float32 [2048, 1152], P(('grp', 'blk'))
All inputs are finite; a program needn't handle non-finite values.
Results may differ from a plain program's by a relative error of at most 0.0095.
Values may be sent and summed in bfloat16 or wider, within the bound.
A program may use at most 64 MiB of HBM per device.

v0:
```python
import math

import jax
import jax.numpy as jnp
from jax import lax
from jax.sharding import PartitionSpec as P

HEADS = 16


def shifted(array, axis, by):
    devices = lax.axis_size(axis)
    return lax.ppermute(array, axis, [(i, (i + by) % devices) for i in range(devices)])


def head_table(width, heads):
    owner = jnp.arange(width, dtype=jnp.int32) // (width // heads)
    return (owner[:, None] == jnp.arange(heads, dtype=jnp.int32)[None, :]).astype(jnp.float32)


def unit_rows(values):
    inverse = lax.rsqrt(jnp.sum(values * values, axis=1, keepdims=True) + 1e-06)
    return (values * inverse, inverse)


def chain_back(grad_unit, unit_f, inverse):
    inner = jnp.sum(unit_f * grad_unit, axis=1, keepdims=True)
    return (grad_unit - unit_f * inner) * inverse


def pool_weights(scores):
    top = jnp.max(scores, axis=1, keepdims=True)
    expo = jnp.exp(scores - top)
    return expo / jnp.sum(expo, axis=1, keepdims=True)


def cross_rows(left, right):
    return lax.dot_general(
        left, right, (((1,), (1,)), ((), ())), preferred_element_type=jnp.float32
    )


def cross_columns(left, right):
    return lax.dot_general(
        left, right, (((0,), (0,)), ((), ())), preferred_element_type=jnp.float32
    )


def local(patches, probe, w_key, w_value, w_out, texts):
    rows, patch_count, width = patches.shape
    heads = HEADS
    head_size = width // heads
    scaling = 1.0 / math.sqrt(head_size)
    query_table = head_table(width, heads) * probe.astype(jnp.float32)[:, None]
    flat = patches.reshape(rows * patch_count, width)
    columns = flat
    keys = jnp.dot(
        columns,
        lax.all_gather(w_key, "grp", axis=0, tiled=True),
        preferred_element_type=jnp.float32,
    )
    values = jnp.dot(
        columns,
        lax.all_gather(w_value, "grp", axis=0, tiled=True),
        preferred_element_type=jnp.float32,
    )
    scores = (
        jnp.dot(keys, query_table, precision=lax.Precision.HIGHEST).reshape(
            rows, patch_count, heads
        )
        * scaling
    )
    weights = pool_weights(scores)
    pooled = jnp.einsum(
        "rph,rphk->rhk",
        weights,
        values.reshape(rows, patch_count, heads, head_size),
        precision=lax.Precision.HIGHEST,
    ).reshape(rows, width)
    pooled_b = pooled.astype(jnp.bfloat16)
    columns = pooled_b
    embed = jnp.dot(
        columns,
        lax.all_gather(w_out, "grp", axis=0, tiled=True),
        preferred_element_type=jnp.float32,
    )
    unit_image, inverse_image = unit_rows(embed)
    unit_image_b = unit_image.astype(jnp.bfloat16)
    unit_text, inverse_text = unit_rows(texts.astype(jnp.float32))
    unit_text_b = unit_text.astype(jnp.bfloat16)
    cycle = lax.axis_size("blk")
    zero_rows = jnp.zeros((rows, width), jnp.float32)
    diagonal = jnp.eye(rows, dtype=jnp.float32)

    def lap_step(turn, carry):
        visiting, partial_value, grad_unit = carry
        logits = 10.0 * cross_rows(unit_image_b, visiting) - 2.0
        target = diagonal * (turn == 0).astype(jnp.float32)
        slopes = (jax.nn.sigmoid(logits) - target).astype(jnp.bfloat16)
        grad_unit = grad_unit + jnp.dot(slopes, visiting, preferred_element_type=jnp.float32)
        partial_value = partial_value + cross_columns(slopes, unit_image_b)
        visiting = shifted(visiting, "blk", 1)
        partial_value = shifted(partial_value, "blk", 1)
        return (visiting, partial_value, grad_unit)

    _, grad_unit_text, grad_unit_image = lax.fori_loop(
        0, cycle, lap_step, (unit_text_b, zero_rows, zero_rows)
    )
    grad_image = chain_back(10.0 * grad_unit_image, unit_image, inverse_image)
    grad_text = chain_back(10.0 * grad_unit_text, unit_text, inverse_text)
    return (grad_image, grad_text)


def solution(mesh):
    in_specs = (
        P(("grp", "blk"), None, None),
        P(),
        P("grp", None),
        P("grp", None),
        P("grp", None),
        P(("grp", "blk"), None),
    )
    out_specs = (P(("grp", "blk"), None), P(("grp", "blk"), None))
    return jax.shard_map(local, mesh=mesh, in_specs=in_specs, out_specs=out_specs, check_vma=False)
```

profile of v0, /device:TPU:4, one launch (start us, length us, event | category | flops | bytes accessed | tf_op | source)
XLA Modules:
  0.0 269.2 jit_solution(12987428255883348162)
XLA Ops:
  7.2 0.7 all-gather.4.cloned.1.call-update
  8.0 0.7 all-gather.6.cloned.1.call-update
  8.7 0.7 all-gather.8.cloned.1.call-update
  9.4 0.7 convert_element_type.44
  10.1 0.8 fusion.26
  11.0 39.2 %all-gather.4.cloned.1.call-done = bf16[1152,1152]{1,0:T(8,128)(2,1)} async-done(((bf16[72,1152]{1,0:T(8,128)(2,1)}), bf16[1152,1152]{1,0:T(8,128)(2,1)}) %all-gather.4.cloned.1.call-update) | async-done | bytes 2654224 | tf_op jit(solution)/shard_map/all_gather | solution.py:59
  50.2 3.6 %fusion.32 = f32[512,1152]{1,0:T(8,128)S(1)} fusion(bf16[512,1152]{1,0:T(8,128)(2,1)S(1)} %bitcast.43, bf16[1152,1152]{1,0:T(8,128)(2,1)} %all-gather.4.cloned.1.call-done), kind=kOutput, calls=%fused_computation.50 | convolution fusion | flops 1358954496 | bytes 6193152 | tf_op jit(solution)/shard_map/dot_general | solution.py:57
  53.8 2.3 convolution_multiply_fusion.1
  56.2 33.6 %all-gather.6.cloned.1.call-done = bf16[1152,1152]{1,0:T(8,128)(2,1)} async-done(((bf16[72,1152]{1,0:T(8,128)(2,1)}), bf16[1152,1152]{1,0:T(8,128)(2,1)}) %all-gather.6.cloned.1.call-update) | async-done | bytes 2654224 | tf_op jit(solution)/shard_map/all_gather | solution.py:64
  89.8 5.2 %copy.9 = bf16[1152,1152]{0,1:T(8,128)(2,1)} copy(bf16[1152,1152]{1,0:T(8,128)(2,1)} %all-gather.6.cloned.1.call-done) | data formatting | bytes 5308416 | tf_op jit(solution)/shard_map/all_gather | solution.py:64
  95.0 2.5 fusion.31
  97.7 4.6 %fusion.10 = f32[8,64,16,72]{3,1,2,0:T(8,128)S(1)} fusion(bf16[16,72,1152,1]{2,1,0,3:T(8,128)(2,1)} %bitcast.44, bf16[8,64,1152]{2,1,0:T(8,128)(2,1)S(1)} %copy-done), kind=kOutput, calls=%fused_computation.13 | convolution fusion | flops 1358954496 | bytes 6193152 | tf_op jit(solution)/shard_map/dot_general | solution.py:62
  102.4 3.6 %fusion.18 = f32[8,16,1,72]{3,2,1,0:T(1,128)S(1)} fusion(f32[8,64,16,72]{3,1,2,0:T(8,128)S(1)} %fusion.10, f32[8,64,16,1]{1,0,2,3:T(8,128)S(1)} %divide_bitcast_fusion), kind=kOutput, calls=%fused_computation.23 | convolution fusion | flops 7077888 | bytes 2428928 | tf_op jit(solution)/shard_map/rph,rphk->rhk/dot_general | solution.py:74
  106.1 23.3 %all-gather.8.cloned.1.call-done = bf16[1152,1152]{1,0:T(8,128)(2,1)} async-done(((bf16[72,1152]{1,0:T(8,128)(2,1)}), bf16[1152,1152]{1,0:T(8,128)(2,1)}) %all-gather.8.cloned.1.call-update) | async-done | bytes 2654224 | tf_op jit(solution)/shard_map/all_gather | solution.py:84
  129.4 2.3 multiply_reduce_fusion.1
  131.8 129.1 %while.20 = (s32[]{:T(128)}, bf16[8,1152]{1,0:T(8,128)(2,1)S(1)}, f32[8,1152]{1,0:T(8,128)S(1)}, f32[8,1152]{1,0:T(8,128)S(1)}, bf16[8,1152]{1,0:T(8,128)(2,1)S(1)}, /*index=5*/s32[]{:T(128)}, s32[]{:T(128)}) while((s32[]{:T(128)}, bf16[8,1152]{1,0:T(8,128)(2,1)S(1)}, f32[8,1152]{1,0:T(8,128)S(1)}, f32[8,1152]{1,0:T(8,128)S(1)}, ...), condition=%wide.region_5.6_spmd.clone, body=%wide.region_4.5_spmd.clone.sunk | while | flops 470596 | bytes 479792 | solution.py:106
  131.8 1.6 collective-permute-start
  133.8 1.6 collective-permute-start.1
  135.5 3.8 %collective-permute-done = bf16[8,1152]{1,0:T(8,128)(2,1)S(1)} collective-permute-done((bf16[8,1152]{1,0:T(8,128)(2,1)S(1)}, bf16[8,1152]{1,0:T(8,128)(2,1)S(1)}, u32[]{:S(2)}, u32[]{:S(2)}) %collective-permute-start) | collective-permute-done | bytes 18464 | tf_op jit(solution)/shard_map/while/body/eval_jaxpr/ppermute | solution.py:13
  139.3 2.1 collective-permute-done.1
  141.9 6.9 %collective-permute-done = bf16[8,1152]{1,0:T(8,128)(2,1)S(1)} collective-permute-done((bf16[8,1152]{1,0:T(8,128)(2,1)S(1)}, bf16[8,1152]{1,0:T(8,128)(2,1)S(1)}, u32[]{:S(2)}, u32[]{:S(2)}) %collective-permute-start) | collective-permute-done | bytes 18464 | tf_op jit(solution)/shard_map/while/body/eval_jaxpr/ppermute | solution.py:13
  148.8 0.5 collective-permute-done.1
  149.8 6.9 %collective-permute-done = bf16[8,1152]{1,0:T(8,128)(2,1)S(1)} collective-permute-done((bf16[8,1152]{1,0:T(8,128)(2,1)S(1)}, bf16[8,1152]{1,0:T(8,128)(2,1)S(1)}, u32[]{:S(2)}, u32[]{:S(2)}) %collective-permute-start) | collective-permute-done | bytes 18464 | tf_op jit(solution)/shard_map/while/body/eval_jaxpr/ppermute | solution.py:13
  156.7 0.5 collective-permute-done.1
  157.7 6.9 %collective-permute-done = bf16[8,1152]{1,0:T(8,128)(2,1)S(1)} collective-permute-done((bf16[8,1152]{1,0:T(8,128)(2,1)S(1)}, bf16[8,1152]{1,0:T(8,128)(2,1)S(1)}, u32[]{:S(2)}, u32[]{:S(2)}) %collective-permute-start) | collective-permute-done | bytes 18464 | tf_op jit(solution)/shard_map/while/body/eval_jaxpr/ppermute | solution.py:13
  164.6 0.5 collective-permute-done.1
  165.6 6.9 %collective-permute-done = bf16[8,1152]{1,0:T(8,128)(2,1)S(1)} collective-permute-done((bf16[8,1152]{1,0:T(8,128)(2,1)S(1)}, bf16[8,1152]{1,0:T(8,128)(2,1)S(1)}, u32[]{:S(2)}, u32[]{:S(2)}) %collective-permute-start) | collective-permute-done | bytes 18464 | tf_op jit(solution)/shard_map/while/body/eval_jaxpr/ppermute | solution.py:13
  172.5 0.5 collective-permute-done.1
  173.5 7.1 %collective-permute-done = bf16[8,1152]{1,0:T(8,128)(2,1)S(1)} collective-permute-done((bf16[8,1152]{1,0:T(8,128)(2,1)S(1)}, bf16[8,1152]{1,0:T(8,128)(2,1)S(1)}, u32[]{:S(2)}, u32[]{:S(2)}) %collective-permute-start) | collective-permute-done | bytes 18464 | tf_op jit(solution)/shard_map/while/body/eval_jaxpr/ppermute | solution.py:13
  180.6 0.8 collective-permute-done.1
  181.9 6.9 %collective-permute-done = bf16[8,1152]{1,0:T(8,128)(2,1)S(1)} collective-permute-done((bf16[8,1152]{1,0:T(8,128)(2,1)S(1)}, bf16[8,1152]{1,0:T(8,128)(2,1)S(1)}, u32[]{:S(2)}, u32[]{:S(2)}) %collective-permute-start) | collective-permute-done | bytes 18464 | tf_op jit(solution)/shard_map/while/body/eval_jaxpr/ppermute | solution.py:13
  188.8 0.5 collective-permute-done.1
  189.8 6.9 %collective-permute-done = bf16[8,1152]{1,0:T(8,128)(2,1)S(1)} collective-permute-done((bf16[8,1152]{1,0:T(8,128)(2,1)S(1)}, bf16[8,1152]{1,0:T(8,128)(2,1)S(1)}, u32[]{:S(2)}, u32[]{:S(2)}) %collective-permute-start) | collective-permute-done | bytes 18464 | tf_op jit(solution)/shard_map/while/body/eval_jaxpr/ppermute | solution.py:13
  196.7 0.5 collective-permute-done.1
  197.7 6.9 %collective-permute-done = bf16[8,1152]{1,0:T(8,128)(2,1)S(1)} collective-permute-done((bf16[8,1152]{1,0:T(8,128)(2,1)S(1)}, bf16[8,1152]{1,0:T(8,128)(2,1)S(1)}, u32[]{:S(2)}, u32[]{:S(2)}) %collective-permute-start) | collective-permute-done | bytes 18464 | tf_op jit(solution)/shard_map/while/body/eval_jaxpr/ppermute | solution.py:13
  204.6 0.5 collective-permute-done.1
  205.7 6.9 %collective-permute-done = bf16[8,1152]{1,0:T(8,128)(2,1)S(1)} collective-permute-done((bf16[8,1152]{1,0:T(8,128)(2,1)S(1)}, bf16[8,1152]{1,0:T(8,128)(2,1)S(1)}, u32[]{:S(2)}, u32[]{:S(2)}) %collective-permute-start) | collective-permute-done | bytes 18464 | tf_op jit(solution)/shard_map/while/body/eval_jaxpr/ppermute | solution.py:13
  212.6 0.5 collective-permute-done.1
  213.6 6.9 %collective-permute-done = bf16[8,1152]{1,0:T(8,128)(2,1)S(1)} collective-permute-done((bf16[8,1152]{1,0:T(8,128)(2,1)S(1)}, bf16[8,1152]{1,0:T(8,128)(2,1)S(1)}, u32[]{:S(2)}, u32[]{:S(2)}) %collective-permute-start) | collective-permute-done | bytes 18464 | tf_op jit(solution)/shard_map/while/body/eval_jaxpr/ppermute | solution.py:13
  220.5 0.5 collective-permute-done.1
  221.5 6.9 %collective-permute-done = bf16[8,1152]{1,0:T(8,128)(2,1)S(1)} collective-permute-done((bf16[8,1152]{1,0:T(8,128)(2,1)S(1)}, bf16[8,1152]{1,0:T(8,128)(2,1)S(1)}, u32[]{:S(2)}, u32[]{:S(2)}) %collective-permute-start) | collective-permute-done | bytes 18464 | tf_op jit(solution)/shard_map/while/body/eval_jaxpr/ppermute | solution.py:13
  228.4 0.8 collective-permute-done.1
  229.7 6.9 %collective-permute-done = bf16[8,1152]{1,0:T(8,128)(2,1)S(1)} collective-permute-done((bf16[8,1152]{1,0:T(8,128)(2,1)S(1)}, bf16[8,1152]{1,0:T(8,128)(2,1)S(1)}, u32[]{:S(2)}, u32[]{:S(2)}) %collective-permute-start) | collective-permute-done | bytes 18464 | tf_op jit(solution)/shard_map/while/body/eval_jaxpr/ppermute | solution.py:13
  237.7 6.9 %collective-permute-done = bf16[8,1152]{1,0:T(8,128)(2,1)S(1)} collective-permute-done((bf16[8,1152]{1,0:T(8,128)(2,1)S(1)}, bf16[8,1152]{1,0:T(8,128)(2,1)S(1)}, u32[]{:S(2)}, u32[]{:S(2)}) %collective-permute-start) | collective-permute-done | bytes 18464 | tf_op jit(solution)/shard_map/while/body/eval_jaxpr/ppermute | solution.py:13
  245.6 6.9 %collective-permute-done = bf16[8,1152]{1,0:T(8,128)(2,1)S(1)} collective-permute-done((bf16[8,1152]{1,0:T(8,128)(2,1)S(1)}, bf16[8,1152]{1,0:T(8,128)(2,1)S(1)}, u32[]{:S(2)}, u32[]{:S(2)}) %collective-permute-start) | collective-permute-done | bytes 18464 | tf_op jit(solution)/shard_map/while/body/eval_jaxpr/ppermute | solution.py:13
  253.5 6.9 %collective-permute-done = bf16[8,1152]{1,0:T(8,128)(2,1)S(1)} collective-permute-done((bf16[8,1152]{1,0:T(8,128)(2,1)S(1)}, bf16[8,1152]{1,0:T(8,128)(2,1)S(1)}, u32[]{:S(2)}, u32[]{:S(2)}) %collective-permute-start) | collective-permute-done | bytes 18464 | tf_op jit(solution)/shard_map/while/body/eval_jaxpr/ppermute | solution.py:13
  261.1 0.7 fusion.25
  262.0 0.7 subtract_multiply_fusion
  (117 shorter events, 10.5 us)
Async XLA Ops:
  7.2 43.0 %copy-start = (bf16[8,64,1152]{2,1,0:T(8,128)(2,1)S(1)}, bf16[8,64,1152]{2,1,0:T(8,128)(2,1)}, u32[]{:S(2)}) copy-start(bf16[8,64,1152]{2,1,0:T(8,128)(2,1)} %param.8) | copy-start | bytes 3538948
  7.2 43.0 %all-gather.4.cloned.1.call-start = ((), (), s32[]{:S(2)}) async-start(), calls=%async_computation | async-start | bytes 2820096 | tf_op jit(solution)/shard_map/all_gather | solution.py:59
  7.9 81.9 %all-gather.6.cloned.1.call-start = ((), (), s32[]{:S(2)}) async-start(), calls=%async_computation.1 | async-start | bytes 2820096 | tf_op jit(solution)/shard_map/all_gather | solution.py:64
  8.7 120.7 %all-gather.8.cloned.1.call-start = ((), (), s32[]{:S(2)}) async-start(), calls=%async_computation.2 | async-start | bytes 2820096 | tf_op jit(solution)/shard_map/all_gather | solution.py:84
  102.3 29.4 %copy-start.1 = (bf16[8,1152]{1,0:T(8,128)(2,1)S(1)}, bf16[8,1152]{1,0:T(8,128)(2,1)}, u32[]{:S(2)}) copy-start(bf16[8,1152]{1,0:T(8,128)(2,1)} %param.13) | copy-start | bytes 55300
  131.8 7.5 %collective-permute-start = (bf16[8,1152]{1,0:T(8,128)(2,1)S(1)}, bf16[8,1152]{1,0:T(8,128)(2,1)S(1)}, u32[]{:S(2)}, u32[]{:S(2)}) collective-permute-start(bf16[8,1152]{1,0:T(8,128)(2,1)S(1)} %copy.20), channel_id=1, source_target_pairs={{0,1},{1,2},{2,3},{3,4},{4,5},{5,6},{6,7},{7,8},{8,9},{9,10},{10,1... | collective-permute-start | bytes 55304 | tf_op jit(solution)/shard_map/while/body/eval_jaxpr/ppermute | solution.py:13
  133.8 7.6 %collective-permute-start.1 = (f32[8,1152]{1,0:T(8,128)S(1)}, f32[8,1152]{1,0:T(8,128)S(1)}, u32[]{:S(2)}, u32[]{:S(2)}) collective-permute-start(f32[8,1152]{1,0:T(8,128)S(1)} %convolution_add_fusion.4), channel_id=1, source_target_pairs={{0,1},{1,2},{2,3},{3,4},{4,5},{5,6},{6,7},{7,8},{8,9},{9,10},{10,1... | collective-permute-start | bytes 110600 | tf_op jit(solution)/shard_map/while/body/eval_jaxpr/ppermute | solution.py:13
  141.4 7.4 %collective-permute-start = (bf16[8,1152]{1,0:T(8,128)(2,1)S(1)}, bf16[8,1152]{1,0:T(8,128)(2,1)S(1)}, u32[]{:S(2)}, u32[]{:S(2)}) collective-permute-start(bf16[8,1152]{1,0:T(8,128)(2,1)S(1)} %copy.20), channel_id=1, source_target_pairs={{0,1},{1,2},{2,3},{3,4},{4,5},{5,6},{6,7},{7,8},{8,9},{9,10},{10,1... | collective-permute-start | bytes 55304 | tf_op jit(solution)/shard_map/while/body/eval_jaxpr/ppermute | solution.py:13
  141.7 7.6 %collective-permute-start.1 = (f32[8,1152]{1,0:T(8,128)S(1)}, f32[8,1152]{1,0:T(8,128)S(1)}, u32[]{:S(2)}, u32[]{:S(2)}) collective-permute-start(f32[8,1152]{1,0:T(8,128)S(1)} %convolution_add_fusion.4), channel_id=1, source_target_pairs={{0,1},{1,2},{2,3},{3,4},{4,5},{5,6},{6,7},{7,8},{8,9},{9,10},{10,1... | collective-permute-start | bytes 110600 | tf_op jit(solution)/shard_map/while/body/eval_jaxpr/ppermute | solution.py:13
  149.3 7.4 %collective-permute-start = (bf16[8,1152]{1,0:T(8,128)(2,1)S(1)}, bf16[8,1152]{1,0:T(8,128)(2,1)S(1)}, u32[]{:S(2)}, u32[]{:S(2)}) collective-permute-start(bf16[8,1152]{1,0:T(8,128)(2,1)S(1)} %copy.20), channel_id=1, source_target_pairs={{0,1},{1,2},{2,3},{3,4},{4,5},{5,6},{6,7},{7,8},{8,9},{9,10},{10,1... | collective-permute-start | bytes 55304 | tf_op jit(solution)/shard_map/while/body/eval_jaxpr/ppermute | solution.py:13
  149.6 7.6 %collective-permute-start.1 = (f32[8,1152]{1,0:T(8,128)S(1)}, f32[8,1152]{1,0:T(8,128)S(1)}, u32[]{:S(2)}, u32[]{:S(2)}) collective-permute-start(f32[8,1152]{1,0:T(8,128)S(1)} %convolution_add_fusion.4), channel_id=1, source_target_pairs={{0,1},{1,2},{2,3},{3,4},{4,5},{5,6},{6,7},{7,8},{8,9},{9,10},{10,1... | collective-permute-start | bytes 110600 | tf_op jit(solution)/shard_map/while/body/eval_jaxpr/ppermute | solution.py:13
  157.2 7.4 %collective-permute-start = (bf16[8,1152]{1,0:T(8,128)(2,1)S(1)}, bf16[8,1152]{1,0:T(8,128)(2,1)S(1)}, u32[]{:S(2)}, u32[]{:S(2)}) collective-permute-start(bf16[8,1152]{1,0:T(8,128)(2,1)S(1)} %copy.20), channel_id=1, source_target_pairs={{0,1},{1,2},{2,3},{3,4},{4,5},{5,6},{6,7},{7,8},{8,9},{9,10},{10,1... | collective-permute-start | bytes 55304 | tf_op jit(solution)/shard_map/while/body/eval_jaxpr/ppermute | solution.py:13
  157.6 7.6 %collective-permute-start.1 = (f32[8,1152]{1,0:T(8,128)S(1)}, f32[8,1152]{1,0:T(8,128)S(1)}, u32[]{:S(2)}, u32[]{:S(2)}) collective-permute-start(f32[8,1152]{1,0:T(8,128)S(1)} %convolution_add_fusion.4), channel_id=1, source_target_pairs={{0,1},{1,2},{2,3},{3,4},{4,5},{5,6},{6,7},{7,8},{8,9},{9,10},{10,1... | collective-permute-start | bytes 110600 | tf_op jit(solution)/shard_map/while/body/eval_jaxpr/ppermute | solution.py:13
  165.2 7.4 %collective-permute-start = (bf16[8,1152]{1,0:T(8,128)(2,1)S(1)}, bf16[8,1152]{1,0:T(8,128)(2,1)S(1)}, u32[]{:S(2)}, u32[]{:S(2)}) collective-permute-start(bf16[8,1152]{1,0:T(8,128)(2,1)S(1)} %copy.20), channel_id=1, source_target_pairs={{0,1},{1,2},{2,3},{3,4},{4,5},{5,6},{6,7},{7,8},{8,9},{9,10},{10,1... | collective-permute-start | bytes 55304 | tf_op jit(solution)/shard_map/while/body/eval_jaxpr/ppermute | solution.py:13
  165.5 7.6 %collective-permute-start.1 = (f32[8,1152]{1,0:T(8,128)S(1)}, f32[8,1152]{1,0:T(8,128)S(1)}, u32[]{:S(2)}, u32[]{:S(2)}) collective-permute-start(f32[8,1152]{1,0:T(8,128)S(1)} %convolution_add_fusion.4), channel_id=1, source_target_pairs={{0,1},{1,2},{2,3},{3,4},{4,5},{5,6},{6,7},{7,8},{8,9},{9,10},{10,1... | collective-permute-start | bytes 110600 | tf_op jit(solution)/shard_map/while/body/eval_jaxpr/ppermute | solution.py:13
  173.1 7.6 %collective-permute-start = (bf16[8,1152]{1,0:T(8,128)(2,1)S(1)}, bf16[8,1152]{1,0:T(8,128)(2,1)S(1)}, u32[]{:S(2)}, u32[]{:S(2)}) collective-permute-start(bf16[8,1152]{1,0:T(8,128)(2,1)S(1)} %copy.20), channel_id=1, source_target_pairs={{0,1},{1,2},{2,3},{3,4},{4,5},{5,6},{6,7},{7,8},{8,9},{9,10},{10,1... | collective-permute-start | bytes 55304 | tf_op jit(solution)/shard_map/while/body/eval_jaxpr/ppermute | solution.py:13
  173.4 8.0 %collective-permute-start.1 = (f32[8,1152]{1,0:T(8,128)S(1)}, f32[8,1152]{1,0:T(8,128)S(1)}, u32[]{:S(2)}, u32[]{:S(2)}) collective-permute-start(f32[8,1152]{1,0:T(8,128)S(1)} %convolution_add_fusion.4), channel_id=1, source_target_pairs={{0,1},{1,2},{2,3},{3,4},{4,5},{5,6},{6,7},{7,8},{8,9},{9,10},{10,1... | collective-permute-start | bytes 110600 | tf_op jit(solution)/shard_map/while/body/eval_jaxpr/ppermute | solution.py:13
  181.4 7.4 %collective-permute-start = (bf16[8,1152]{1,0:T(8,128)(2,1)S(1)}, bf16[8,1152]{1,0:T(8,128)(2,1)S(1)}, u32[]{:S(2)}, u32[]{:S(2)}) collective-permute-start(bf16[8,1152]{1,0:T(8,128)(2,1)S(1)} %copy.20), channel_id=1, source_target_pairs={{0,1},{1,2},{2,3},{3,4},{4,5},{5,6},{6,7},{7,8},{8,9},{9,10},{10,1... | collective-permute-start | bytes 55304 | tf_op jit(solution)/shard_map/while/body/eval_jaxpr/ppermute | solution.py:13
  181.8 7.6 %collective-permute-start.1 = (f32[8,1152]{1,0:T(8,128)S(1)}, f32[8,1152]{1,0:T(8,128)S(1)}, u32[]{:S(2)}, u32[]{:S(2)}) collective-permute-start(f32[8,1152]{1,0:T(8,128)S(1)} %convolution_add_fusion.4), channel_id=1, source_target_pairs={{0,1},{1,2},{2,3},{3,4},{4,5},{5,6},{6,7},{7,8},{8,9},{9,10},{10,1... | collective-permute-start | bytes 110600 | tf_op jit(solution)/shard_map/while/body/eval_jaxpr/ppermute | solution.py:13
  189.3 7.4 %collective-permute-start = (bf16[8,1152]{1,0:T(8,128)(2,1)S(1)}, bf16[8,1152]{1,0:T(8,128)(2,1)S(1)}, u32[]{:S(2)}, u32[]{:S(2)}) collective-permute-start(bf16[8,1152]{1,0:T(8,128)(2,1)S(1)} %copy.20), channel_id=1, source_target_pairs={{0,1},{1,2},{2,3},{3,4},{4,5},{5,6},{6,7},{7,8},{8,9},{9,10},{10,1... | collective-permute-start | bytes 55304 | tf_op jit(solution)/shard_map/while/body/eval_jaxpr/ppermute | solution.py:13
  189.7 7.6 %collective-permute-start.1 = (f32[8,1152]{1,0:T(8,128)S(1)}, f32[8,1152]{1,0:T(8,128)S(1)}, u32[]{:S(2)}, u32[]{:S(2)}) collective-permute-start(f32[8,1152]{1,0:T(8,128)S(1)} %convolution_add_fusion.4), channel_id=1, source_target_pairs={{0,1},{1,2},{2,3},{3,4},{4,5},{5,6},{6,7},{7,8},{8,9},{9,10},{10,1... | collective-permute-start | bytes 110600 | tf_op jit(solution)/shard_map/while/body/eval_jaxpr/ppermute | solution.py:13
  197.3 7.4 %collective-permute-start = (bf16[8,1152]{1,0:T(8,128)(2,1)S(1)}, bf16[8,1152]{1,0:T(8,128)(2,1)S(1)}, u32[]{:S(2)}, u32[]{:S(2)}) collective-permute-start(bf16[8,1152]{1,0:T(8,128)(2,1)S(1)} %copy.20), channel_id=1, source_target_pairs={{0,1},{1,2},{2,3},{3,4},{4,5},{5,6},{6,7},{7,8},{8,9},{9,10},{10,1... | collective-permute-start | bytes 55304 | tf_op jit(solution)/shard_map/while/body/eval_jaxpr/ppermute | solution.py:13
  197.6 7.6 %collective-permute-start.1 = (f32[8,1152]{1,0:T(8,128)S(1)}, f32[8,1152]{1,0:T(8,128)S(1)}, u32[]{:S(2)}, u32[]{:S(2)}) collective-permute-start(f32[8,1152]{1,0:T(8,128)S(1)} %convolution_add_fusion.4), channel_id=1, source_target_pairs={{0,1},{1,2},{2,3},{3,4},{4,5},{5,6},{6,7},{7,8},{8,9},{9,10},{10,1... | collective-permute-start | bytes 110600 | tf_op jit(solution)/shard_map/while/body/eval_jaxpr/ppermute | solution.py:13
  205.2 7.4 %collective-permute-start = (bf16[8,1152]{1,0:T(8,128)(2,1)S(1)}, bf16[8,1152]{1,0:T(8,128)(2,1)S(1)}, u32[]{:S(2)}, u32[]{:S(2)}) collective-permute-start(bf16[8,1152]{1,0:T(8,128)(2,1)S(1)} %copy.20), channel_id=1, source_target_pairs={{0,1},{1,2},{2,3},{3,4},{4,5},{5,6},{6,7},{7,8},{8,9},{9,10},{10,1... | collective-permute-start | bytes 55304 | tf_op jit(solution)/shard_map/while/body/eval_jaxpr/ppermute | solution.py:13
  205.5 7.6 %collective-permute-start.1 = (f32[8,1152]{1,0:T(8,128)S(1)}, f32[8,1152]{1,0:T(8,128)S(1)}, u32[]{:S(2)}, u32[]{:S(2)}) collective-permute-start(f32[8,1152]{1,0:T(8,128)S(1)} %convolution_add_fusion.4), channel_id=1, source_target_pairs={{0,1},{1,2},{2,3},{3,4},{4,5},{5,6},{6,7},{7,8},{8,9},{9,10},{10,1... | collective-permute-start | bytes 110600 | tf_op jit(solution)/shard_map/while/body/eval_jaxpr/ppermute | solution.py:13
  213.1 7.4 %collective-permute-start = (bf16[8,1152]{1,0:T(8,128)(2,1)S(1)}, bf16[8,1152]{1,0:T(8,128)(2,1)S(1)}, u32[]{:S(2)}, u32[]{:S(2)}) collective-permute-start(bf16[8,1152]{1,0:T(8,128)(2,1)S(1)} %copy.20), channel_id=1, source_target_pairs={{0,1},{1,2},{2,3},{3,4},{4,5},{5,6},{6,7},{7,8},{8,9},{9,10},{10,1... | collective-permute-start | bytes 55304 | tf_op jit(solution)/shard_map/while/body/eval_jaxpr/ppermute | solution.py:13
  213.4 7.6 %collective-permute-start.1 = (f32[8,1152]{1,0:T(8,128)S(1)}, f32[8,1152]{1,0:T(8,128)S(1)}, u32[]{:S(2)}, u32[]{:S(2)}) collective-permute-start(f32[8,1152]{1,0:T(8,128)S(1)} %convolution_add_fusion.4), channel_id=1, source_target_pairs={{0,1},{1,2},{2,3},{3,4},{4,5},{5,6},{6,7},{7,8},{8,9},{9,10},{10,1... | collective-permute-start | bytes 110600 | tf_op jit(solution)/shard_map/while/body/eval_jaxpr/ppermute | solution.py:13
  221.0 7.4 %collective-permute-start = (bf16[8,1152]{1,0:T(8,128)(2,1)S(1)}, bf16[8,1152]{1,0:T(8,128)(2,1)S(1)}, u32[]{:S(2)}, u32[]{:S(2)}) collective-permute-start(bf16[8,1152]{1,0:T(8,128)(2,1)S(1)} %copy.20), channel_id=1, source_target_pairs={{0,1},{1,2},{2,3},{3,4},{4,5},{5,6},{6,7},{7,8},{8,9},{9,10},{10,1... | collective-permute-start | bytes 55304 | tf_op jit(solution)/shard_map/while/body/eval_jaxpr/ppermute | solution.py:13
  221.3 7.9 %collective-permute-start.1 = (f32[8,1152]{1,0:T(8,128)S(1)}, f32[8,1152]{1,0:T(8,128)S(1)}, u32[]{:S(2)}, u32[]{:S(2)}) collective-permute-start(f32[8,1152]{1,0:T(8,128)S(1)} %convolution_add_fusion.4), channel_id=1, source_target_pairs={{0,1},{1,2},{2,3},{3,4},{4,5},{5,6},{6,7},{7,8},{8,9},{9,10},{10,1... | collective-permute-start | bytes 110600 | tf_op jit(solution)/shard_map/while/body/eval_jaxpr/ppermute | solution.py:13
  229.3 7.4 %collective-permute-start = (bf16[8,1152]{1,0:T(8,128)(2,1)S(1)}, bf16[8,1152]{1,0:T(8,128)(2,1)S(1)}, u32[]{:S(2)}, u32[]{:S(2)}) collective-permute-start(bf16[8,1152]{1,0:T(8,128)(2,1)S(1)} %copy.20), channel_id=1, source_target_pairs={{0,1},{1,2},{2,3},{3,4},{4,5},{5,6},{6,7},{7,8},{8,9},{9,10},{10,1... | collective-permute-start | bytes 55304 | tf_op jit(solution)/shard_map/while/body/eval_jaxpr/ppermute | solution.py:13
  229.6 7.6 %collective-permute-start.1 = (f32[8,1152]{1,0:T(8,128)S(1)}, f32[8,1152]{1,0:T(8,128)S(1)}, u32[]{:S(2)}, u32[]{:S(2)}) collective-permute-start(f32[8,1152]{1,0:T(8,128)S(1)} %convolution_add_fusion.4), channel_id=1, source_target_pairs={{0,1},{1,2},{2,3},{3,4},{4,5},{5,6},{6,7},{7,8},{8,9},{9,10},{10,1... | collective-permute-start | bytes 110600 | tf_op jit(solution)/shard_map/while/body/eval_jaxpr/ppermute | solution.py:13
  237.2 7.4 %collective-permute-start = (bf16[8,1152]{1,0:T(8,128)(2,1)S(1)}, bf16[8,1152]{1,0:T(8,128)(2,1)S(1)}, u32[]{:S(2)}, u32[]{:S(2)}) collective-permute-start(bf16[8,1152]{1,0:T(8,128)(2,1)S(1)} %copy.20), channel_id=1, source_target_pairs={{0,1},{1,2},{2,3},{3,4},{4,5},{5,6},{6,7},{7,8},{8,9},{9,10},{10,1... | collective-permute-start | bytes 55304 | tf_op jit(solution)/shard_map/while/body/eval_jaxpr/ppermute | solution.py:13
  237.5 7.6 %collective-permute-start.1 = (f32[8,1152]{1,0:T(8,128)S(1)}, f32[8,1152]{1,0:T(8,128)S(1)}, u32[]{:S(2)}, u32[]{:S(2)}) collective-permute-start(f32[8,1152]{1,0:T(8,128)S(1)} %convolution_add_fusion.4), channel_id=1, source_target_pairs={{0,1},{1,2},{2,3},{3,4},{4,5},{5,6},{6,7},{7,8},{8,9},{9,10},{10,1... | collective-permute-start | bytes 110600 | tf_op jit(solution)/shard_map/while/body/eval_jaxpr/ppermute | solution.py:13
  245.1 7.4 %collective-permute-start = (bf16[8,1152]{1,0:T(8,128)(2,1)S(1)}, bf16[8,1152]{1,0:T(8,128)(2,1)S(1)}, u32[]{:S(2)}, u32[]{:S(2)}) collective-permute-start(bf16[8,1152]{1,0:T(8,128)(2,1)S(1)} %copy.20), channel_id=1, source_target_pairs={{0,1},{1,2},{2,3},{3,4},{4,5},{5,6},{6,7},{7,8},{8,9},{9,10},{10,1... | collective-permute-start | bytes 55304 | tf_op jit(solution)/shard_map/while/body/eval_jaxpr/ppermute | solution.py:13
  245.4 7.6 %collective-permute-start.1 = (f32[8,1152]{1,0:T(8,128)S(1)}, f32[8,1152]{1,0:T(8,128)S(1)}, u32[]{:S(2)}, u32[]{:S(2)}) collective-permute-start(f32[8,1152]{1,0:T(8,128)S(1)} %convolution_add_fusion.4), channel_id=1, source_target_pairs={{0,1},{1,2},{2,3},{3,4},{4,5},{5,6},{6,7},{7,8},{8,9},{9,10},{10,1... | collective-permute-start | bytes 110600 | tf_op jit(solution)/shard_map/while/body/eval_jaxpr/ppermute | solution.py:13
  253.0 7.4 %collective-permute-start = (bf16[8,1152]{1,0:T(8,128)(2,1)S(1)}, bf16[8,1152]{1,0:T(8,128)(2,1)S(1)}, u32[]{:S(2)}, u32[]{:S(2)}) collective-permute-start(bf16[8,1152]{1,0:T(8,128)(2,1)S(1)} %copy.20), channel_id=1, source_target_pairs={{0,1},{1,2},{2,3},{3,4},{4,5},{5,6},{6,7},{7,8},{8,9},{9,10},{10,1... | collective-permute-start | bytes 55304 | tf_op jit(solution)/shard_map/while/body/eval_jaxpr/ppermute | solution.py:13
  253.3 7.6 %collective-permute-start.1 = (f32[8,1152]{1,0:T(8,128)S(1)}, f32[8,1152]{1,0:T(8,128)S(1)}, u32[]{:S(2)}, u32[]{:S(2)}) collective-permute-start(f32[8,1152]{1,0:T(8,128)S(1)} %convolution_add_fusion.4), channel_id=1, source_target_pairs={{0,1},{1,2},{2,3},{3,4},{4,5},{5,6},{6,7},{7,8},{8,9},{9,10},{10,1... | collective-permute-start | bytes 110600 | tf_op jit(solution)/shard_map/while/body/eval_jaxpr/ppermute | solution.py:13
Sparse Core Ops, SparseCore 0:
  9.9 40.2 all-gather.3
  52.0 37.6 all-gather.5
  91.7 37.6 all-gather.7
where the time goes:
time: 270 us; the launch traced here: 269 us
  waiting for transfers between devices  217 us (80%)
  matrix products  23.7 us (9%)
  between operations  13.8 us (5%)
  other arithmetic  6.12 us (2%)
  local copies, waits for them, and re-layouts  5.47 us (2%)
  starting transfers between devices  3.4 us (1%)
    ppermute x32, waiting for transfers between devices, shifted(): lax.ppermute(array, axis, [(i, (i + by) % devices) for i in range(devices)])  118 us
    all_gather x1, waiting for transfers between devices, local(): lax.all_gather(w_key, 'grp', axis=0, tiled=True)  39.2 us
    all_gather x1, waiting for transfers between devices, local(): lax.all_gather(w_value, 'grp', axis=0, tiled=True)  33.6 us
    all_gather x1, waiting for transfers between devices, local(): lax.all_gather(w_out, 'grp', axis=0, tiled=True)  23.3 us
  transfers between devices with their start and end apart: 35, of which 35 were waited for; matrix products, arithmetic and copies ran while one was open for 12% of the time, Pallas kernels for 0%

commit v1 on v0

v1 whole, which is shorter than its diff:
```python
import math

import jax
import jax.numpy as jnp
from jax import lax
from jax.experimental import pallas as pl
from jax.experimental.pallas import tpu as pltpu
from jax.sharding import PartitionSpec as P

HEADS = 16
MESH = pl.DeviceIdType.MESH
LANES = 128
F32 = jnp.float32
BF16 = jnp.bfloat16


def dot_rows(left, right):
    return lax.dot_general(left, right, (((1,), (1,)), ((), ())), preferred_element_type=F32)


def dot(left, right):
    return lax.dot_general(left, right, (((1,), (0,)), ((), ())), preferred_element_type=F32)


def unit_rows(values):
    inverse = lax.rsqrt(jnp.sum(values * values, axis=1, keepdims=True) + 1e-06)
    return values * inverse, inverse


def chain_back(grad_unit, unit_f, inverse):
    inner = jnp.sum(unit_f * grad_unit, axis=1, keepdims=True)
    return (grad_unit - unit_f * inner) * inverse


def slopes_of(logits, first_row):
    rows, columns = logits.shape
    row = lax.broadcasted_iota(jnp.int32, (rows, columns), 0) + first_row
    column = lax.broadcasted_iota(jnp.int32, (rows, columns), 1)
    target = jnp.where(row == column, 1.0, 0.0)
    return (jax.nn.sigmoid(10.0 * logits - 2.0) - target).astype(BF16)


def kernel(
    n_grp,
    n_blk,
    patches_hbm,
    probe_ref,
    w_key_hbm,
    w_value_hbm,
    w_out_hbm,
    texts_hbm,
    grad_image_ref,
    grad_text_ref,
    patches,
    w_key,
    w_value,
    w_out,
    texts,
    key_send,
    key_all,
    value_send,
    value_all,
    text_send,
    text_all,
    mixed_send,
    mixed_all,
    embed_send,
    embed_all,
    image_send,
    image_all,
    load_sem,
    send_sem,
    recv_sem,
):
    g, b = lax.axis_index("grp"), lax.axis_index("blk")
    rows = texts.shape[0]
    width = texts.shape[1]
    head_size = width // HEADS
    patch_count = patches.shape[0] // rows

    loads = {}
    for index, (name, source, target) in enumerate(
        (
            ("key", w_key_hbm, w_key),
            ("text", texts_hbm, texts),
            ("value", w_value_hbm, w_value),
            ("patches", patches_hbm, patches),
            ("out", w_out_hbm, w_out),
        )
    ):
        loads[name] = pltpu.make_async_copy(source, target, load_sem.at[index])
        loads[name].start()

    def grp_peer(step):
        return jnp.bitwise_xor(g, step)

    def blk_peer(step):
        return jnp.bitwise_xor(b, step)

    barrier = pltpu.get_barrier_semaphore()
    for step in range(1, n_grp):
        pl.semaphore_signal(barrier, inc=1, device_id=(grp_peer(step), b), device_id_type=MESH)
    for step in range(1, n_blk):
        pl.semaphore_signal(barrier, inc=1, device_id=(g, blk_peer(step)), device_id_type=MESH)

    def scatter(phase, source, target, axis, same):
        count = n_grp if axis == "grp" else n_blk
        for step in range(count - 1, 0, -1):
            peer = grp_peer(step) if axis == "grp" else blk_peer(step)
            device = (peer, b) if axis == "grp" else (g, peer)
            pltpu.make_async_remote_copy(
                src_ref=source if same else source.at[peer],
                dst_ref=target.at[g if axis == "grp" else b],
                send_sem=send_sem.at[phase],
                recv_sem=recv_sem.at[phase],
                device_id=device,
                device_id_type=MESH,
            ).start()

    def total_of(phase, target):
        many = target.at[pl.ds(0, target.shape[0] - 1)]
        return pltpu.make_async_remote_copy(
            src_ref=many,
            dst_ref=many,
            send_sem=send_sem.at[phase],
            recv_sem=recv_sem.at[phase],
            device_id=(g, b),
            device_id_type=MESH,
        )

    column = lax.broadcasted_iota(jnp.int32, (HEADS, width), 1)
    head = lax.broadcasted_iota(jnp.int32, (HEADS, width), 0)
    owned = (column >= head * head_size) & (column < (head + 1) * head_size)
    probe = jnp.broadcast_to(probe_ref[...].astype(F32), (HEADS, width))
    query_table = jnp.where(owned, probe, 0.0).astype(BF16)
    loads["key"].wait()
    keys = dot_rows(query_table, w_key[...])
    key_send[...] = jnp.zeros(key_send.shape, F32)
    key_send[:, :head_size] = keys
    key_all[pl.ds(g, 1)] = key_send[...][None]

    loads["text"].wait()
    unit_text, inverse_text = unit_rows(texts[...].astype(F32))
    text_send[...] = unit_text.astype(BF16)
    text_all[pl.ds(b, 1)] = text_send[...][None]

    loads["value"].wait()
    value_f = w_value[...].astype(F32)
    value_send[...] = jnp.zeros(value_send.shape, BF16)
    for h in range(HEADS):
        piece = value_f[:, h * head_size : (h + 1) * head_size]
        value_send[h, :head_size, :head_size] = piece.astype(BF16)
    value_all[pl.ds(g, 1)] = value_send[pl.ds(g, 1)]

    pl.semaphore_wait(barrier, n_grp + n_blk - 2)

    scatter(0, key_send, key_all, "grp", True)
    scatter(1, value_send, value_all, "grp", False)
    scatter(2, text_send, text_all, "blk", True)

    loads["patches"].wait()
    total_of(0, key_all).wait_recv()
    probe_keys = jnp.concatenate([key_all[i][:, :head_size] for i in range(n_grp)], axis=1)
    top_part = probe_keys.astype(BF16)
    rest = probe_keys - top_part.astype(F32)
    mid_part = rest.astype(BF16)
    low_part = (rest - mid_part.astype(F32)).astype(BF16)
    stacked = jnp.concatenate([top_part, mid_part, low_part], axis=0)
    parts = dot_rows(stacked, patches[...])
    scores = (parts[:HEADS] + parts[HEADS : 2 * HEADS] + parts[2 * HEADS :]) * (
        1.0 / math.sqrt(head_size)
    )
    flat = rows * patch_count
    spread = jnp.broadcast_to(scores[:, None, :], (HEADS, rows, flat)).reshape(HEADS * rows, flat)
    image = lax.broadcasted_iota(jnp.int32, (HEADS, rows, flat), 1).reshape(HEADS * rows, flat)
    position = lax.broadcasted_iota(jnp.int32, (HEADS * rows, flat), 1)
    inside = (position >= image * patch_count) & (position < (image + 1) * patch_count)
    spread = jnp.where(inside, spread, -jnp.inf)
    expo = jnp.exp(spread - jnp.max(spread, axis=1, keepdims=True)).astype(BF16)
    denominator = jnp.sum(expo.astype(F32), axis=1, keepdims=True)
    mixed = dot(expo, patches[...]) / denominator
    mixed_send[...] = mixed.reshape(HEADS, rows, width).astype(BF16)
    mixed_all[pl.ds(g, 1)] = mixed_send[pl.ds(g, 1)]
    scatter(3, mixed_send, mixed_all, "grp", False)

    total_of(1, value_all).wait_recv()
    value_head = value_all[...][:, :head_size, :].astype(F32).reshape(width, LANES).astype(BF16)
    loads["out"].wait()
    total_of(3, mixed_all).wait_recv()
    mixed_head = mixed_all[...].astype(F32).reshape(n_grp * rows, width).astype(BF16)
    pooled = dot(mixed_head, value_head)[:, :head_size].astype(BF16)
    partial_embed = dot(pooled, w_out[...])
    embed_send[...] = partial_embed.reshape(n_grp, rows, width).astype(BF16)
    embed_all[pl.ds(g, 1)] = embed_send[pl.ds(g, 1)]
    scatter(4, embed_send, embed_all, "grp", False)

    total_of(2, text_all).wait_recv()
    all_texts = text_all[...].astype(F32).reshape(n_blk * rows, width).astype(BF16)
    total_of(4, embed_all).wait_recv()
    embed = jnp.sum(embed_all[...].astype(F32), axis=0)
    unit_image, inverse_image = unit_rows(embed)
    unit_image_b = unit_image.astype(BF16)
    image_send[...] = unit_image_b
    image_all[pl.ds(b, 1)] = unit_image_b[None]
    scatter(5, image_send, image_all, "blk", True)

    slopes = slopes_of(dot_rows(unit_image_b, all_texts), b * rows)
    grad_image_ref[...] = chain_back(10.0 * dot(slopes, all_texts), unit_image, inverse_image)

    total_of(5, image_all).wait_recv()
    all_images = image_all[...].astype(F32).reshape(n_blk * rows, width).astype(BF16)
    slopes = slopes_of(dot_rows(text_send[...], all_images), b * rows)
    grad_text_ref[...] = chain_back(10.0 * dot(slopes, all_images), unit_text, inverse_text)

    for phase, target in enumerate((key_all, value_all, text_all, mixed_all, embed_all, image_all)):
        total_of(phase, target).wait_send()


def solution(mesh):
    n_grp, n_blk = mesh.shape["grp"], mesh.shape["blk"]

    def local(patches, probe, w_key, w_value, w_out, texts):
        rows, patch_count, width = patches.shape
        depth = w_key.shape[0]
        padded = -(-depth // 16) * 16
        hbm = pl.BlockSpec(memory_space=pltpu.HBM)
        vmem = pl.BlockSpec(memory_space=pltpu.VMEM)
        out = jax.ShapeDtypeStruct((rows, width), F32)
        return pl.pallas_call(
            lambda *refs: kernel(n_grp, n_blk, *refs),
            out_shape=(out, out),
            in_specs=[hbm, vmem, hbm, hbm, hbm, hbm],
            out_specs=(vmem, vmem),
            scratch_shapes=[
                pltpu.VMEM((rows * patch_count, width), BF16),
                pltpu.VMEM((depth, width), BF16),
                pltpu.VMEM((depth, width), BF16),
                pltpu.VMEM((depth, width), BF16),
                pltpu.VMEM((rows, width), BF16),
                pltpu.VMEM((HEADS, LANES), F32),
                pltpu.VMEM((n_grp, HEADS, LANES), F32),
                pltpu.VMEM((n_grp, padded, LANES), BF16),
                pltpu.VMEM((n_grp, padded, LANES), BF16),
                pltpu.VMEM((rows, width), BF16),
                pltpu.VMEM((n_blk, rows, width), BF16),
                pltpu.VMEM((n_grp, rows, width), BF16),
                pltpu.VMEM((n_grp, rows, width), BF16),
                pltpu.VMEM((n_grp, rows, width), BF16),
                pltpu.VMEM((n_grp, rows, width), BF16),
                pltpu.VMEM((rows, width), BF16),
                pltpu.VMEM((n_blk, rows, width), BF16),
                pltpu.SemaphoreType.DMA((5,)),
                pltpu.SemaphoreType.DMA((6,)),
                pltpu.SemaphoreType.DMA((6,)),
            ],
            compiler_params=pltpu.CompilerParams(
                collective_id=0, has_side_effects=True, vmem_limit_bytes=56 << 20
            ),
        )(patches.reshape(rows * patch_count, width), probe.reshape(1, width), w_key, w_value, w_out, texts)

    split = P(("grp", "blk"), None)
    in_specs = (P(("grp", "blk"), None, None), P(), P("grp", None), P("grp", None), P("grp", None), split)
    return jax.shard_map(local, mesh=mesh, in_specs=in_specs, out_specs=(split, split), check_vma=False)
```

time: 270 us -> 45 us (0.17)
  the two profiles are of different devices: /device:TPU:4 before, /device:TPU:2 now
where the time goes in v1:
time: 45 us; the launch traced here: 44.7 us
  Pallas kernels  40 us (89%)
  local copies, waits for them, and re-layouts  4.06 us (9%)
  between operations  0.64 us (1%)
    pallas_call x1, Pallas kernels, local(): pl.pallas_call(lambda *refs: kernel(n_grp, n_blk, *refs), out_shape=(out,...  40 us
    unnamed x2, local copies, waits for them, and re-layouts  2.77 us
    reshape x1, local copies, waits for them, and re-layouts, local(): probe.reshape(1, width)  1.28 us

profile of v1, /device:TPU:2, one launch (start us, length us, event | category | flops | bytes accessed | tf_op | source)
XLA Modules:
  0.0 44.7 jit_solution(7377318447191183884)
XLA Ops:
  0.6 1.3 %reshape.11.refs_1_ = bf16[1,1152]{1,0:T(2,128)(2,1)} reshape(bf16[1152]{0:T(1024)(128)(2,1)} %param.7) | data formatting | bytes 4608 | tf_op jit(solution)/shard_map/reshape | solution.py:259
  1.9 40.0 %shard_map.77 = (f32[8,1152]{1,0:T(8,128)}, f32[8,1152]{1,0:T(8,128)}) custom-call(bf16[512,1152]{1,0:T(8,128)(2,1)} %bitcast.1, bf16[1,1152]{1,0:T(2,128)(2,1)} %reshape.11.refs_1_, bf16[72,1152]{1,0:T(8,128)(2,1)} %refs_2_.1, bf16[72,1152]{1,0:T(8,128)(2,1)} %refs_3_.1, bf16[72,1152]{1,0:T(8,128)(2,1)} %refs_4_.1, bf16[8,1152]{1,0:T(8,128)(2,1)} %refs_5_.1), custom_call_target="tpu_custom_call" | custom-call | tf_op jit(solution)/shard_map/pallas_call | solution.py:229
  41.9 1.4 %copy.10 = f32[8,1152]{1,0:T(8,128)} copy(f32[8,1152]{1,0:T(8,128)} %get-tuple-element.4) | data formatting | bytes 73728
  43.3 1.4 %copy.11 = f32[8,1152]{1,0:T(8,128)} copy(f32[8,1152]{1,0:T(8,128)} %get-tuple-element.5) | data formatting | bytes 73728

commit v2 on v1

--- a/solution.py
+++ b/solution.py
@@ -44,14 +44,14 @@
     n_grp,
     n_blk,
     patches_hbm,
-    probe_ref,
+    probe_hbm,
     w_key_hbm,
     w_value_hbm,
     w_out_hbm,
     texts_hbm,
-    grad_image_ref,
-    grad_text_ref,
+    grads_ref,
     patches,
+    probe_local,
     w_key,
     w_value,
     w_out,
@@ -81,6 +81,7 @@
     loads = {}
     for index, (name, source, target) in enumerate(
         (
+            ("probe", probe_hbm, probe_local),
             ("key", w_key_hbm, w_key),
             ("text", texts_hbm, texts),
             ("value", w_value_hbm, w_value),
@@ -131,7 +132,8 @@
     column = lax.broadcasted_iota(jnp.int32, (HEADS, width), 1)
     head = lax.broadcasted_iota(jnp.int32, (HEADS, width), 0)
     owned = (column >= head * head_size) & (column < (head + 1) * head_size)
-    probe = jnp.broadcast_to(probe_ref[...].astype(F32), (HEADS, width))
+    loads["probe"].wait()
+    probe = jnp.broadcast_to(probe_local[...].astype(F32)[None, :], (HEADS, width))
     query_table = jnp.where(owned, probe, 0.0).astype(BF16)
     loads["key"].wait()
     keys = dot_rows(query_table, w_key[...])
@@ -205,12 +207,12 @@
     scatter(5, image_send, image_all, "blk", True)
 
     slopes = slopes_of(dot_rows(unit_image_b, all_texts), b * rows)
-    grad_image_ref[...] = chain_back(10.0 * dot(slopes, all_texts), unit_image, inverse_image)
+    grads_ref[:rows] = chain_back(10.0 * dot(slopes, all_texts), unit_image, inverse_image)
 
     total_of(5, image_all).wait_recv()
     all_images = image_all[...].astype(F32).reshape(n_blk * rows, width).astype(BF16)
     slopes = slopes_of(dot_rows(text_send[...], all_images), b * rows)
-    grad_text_ref[...] = chain_back(10.0 * dot(slopes, all_images), unit_text, inverse_text)
+    grads_ref[rows:] = chain_back(10.0 * dot(slopes, all_images), unit_text, inverse_text)
 
     for phase, target in enumerate((key_all, value_all, text_all, mixed_all, embed_all, image_all)):
         total_of(phase, target).wait_send()
@@ -225,14 +227,15 @@
         padded = -(-depth // 16) * 16
         hbm = pl.BlockSpec(memory_space=pltpu.HBM)
         vmem = pl.BlockSpec(memory_space=pltpu.VMEM)
-        out = jax.ShapeDtypeStruct((rows, width), F32)
-        return pl.pallas_call(
+        operands = (patches.reshape(rows * patch_count, width), probe, w_key, w_value, w_out, texts)
+        grads = pl.pallas_call(
             lambda *refs: kernel(n_grp, n_blk, *refs),
-            out_shape=(out, out),
-            in_specs=[hbm, vmem, hbm, hbm, hbm, hbm],
-            out_specs=(vmem, vmem),
+            out_shape=pltpu.VMEM((2 * rows, width), F32),
+            in_specs=[hbm] * len(operands),
+            out_specs=vmem,
             scratch_shapes=[
                 pltpu.VMEM((rows * patch_count, width), BF16),
+                pltpu.VMEM((width,), BF16),
                 pltpu.VMEM((depth, width), BF16),
                 pltpu.VMEM((depth, width), BF16),
                 pltpu.VMEM((depth, width), BF16),
@@ -249,14 +252,15 @@
                 pltpu.VMEM((n_grp, rows, width), BF16),
                 pltpu.VMEM((rows, width), BF16),
                 pltpu.VMEM((n_blk, rows, width), BF16),
-                pltpu.SemaphoreType.DMA((5,)),
+                pltpu.SemaphoreType.DMA((6,)),
                 pltpu.SemaphoreType.DMA((6,)),
                 pltpu.SemaphoreType.DMA((6,)),
             ],
             compiler_params=pltpu.CompilerParams(
-                collective_id=0, has_side_effects=True, vmem_limit_bytes=56 << 20
+                collective_id=0, has_side_effects=True, vmem_limit_bytes=24 << 20
             ),
-        )(patches.reshape(rows * patch_count, width), probe.reshape(1, width), w_key, w_value, w_out, texts)
+        )(*(pltpu.with_memory_space_constraint(x, pltpu.HBM) for x in operands))
+        return grads[:rows], grads[rows:]
 
     split = P(("grp", "blk"), None)
     in_specs = (P(("grp", "blk"), None, None), P(), P("grp", None), P("grp", None), P("grp", None), split)

time: 45 us -> 40.3 us (0.90)
  local copies, waits for them, and re-layouts: 4.06 us -> 0.63 us
  Pallas kernels: 40 us -> 38.9 us
    unnamed x2 -> x0, local copies, waits for them, and re-layouts: 2.77 us -> none
    reshape x1 -> x0, local copies, waits for them, and re-layouts: 1.28 us -> none  [local(): probe.reshape(1, width)]
    pallas_call x1, Pallas kernels: 40 us -> 38.9 us  [local(): pl.pallas_call(lambda *refs: kernel(n_grp, n_blk, *refs), out_shape=pltpu...]
    slice x0 -> x1, local copies, waits for them, and re-layouts: none -> 0.63 us  [local(): return (grads[:rows], grads[rows:])]
where the time goes in v2:
time: 40.3 us; the launch traced here: 40.2 us
  Pallas kernels  38.9 us (97%)
  between operations  0.64 us (2%)
  local copies, waits for them, and re-layouts  0.63 us (2%)
    pallas_call x1, Pallas kernels, local(): pl.pallas_call(lambda *refs: kernel(n_grp, n_blk, *refs), out_shape=pltpu...  38.9 us

profile of v2, /device:TPU:2, one launch (start us, length us, event | category | flops | bytes accessed | tf_op | source)
XLA Modules:
  0.0 40.2 jit_solution(8059336558674619205)
XLA Ops:
  0.6 38.9 %shard_map.77 = f32[16,1152]{1,0:T(8,128)S(1)} custom-call(bf16[512,1152]{1,0:T(8,128)(2,1)} %bitcast.1, bf16[1152]{0:T(1024)(128)(2,1)} %refs_1_.1, bf16[72,1152]{1,0:T(8,128)(2,1)} %refs_2_.1, bf16[72,1152]{1,0:T(8,128)(2,1)} %refs_3_.1, bf16[72,1152]{1,0:T(8,128)(2,1)} %refs_4_.1, bf16[8,1152]{1,0:T(8,128)(2,1)} %refs_5_.1), custom_call_target="tpu_custom_call" | custom-call | tf_op jit(solution)/shard_map/pallas_call | solution.py:231
  39.6 0.6 %fusion = (f32[8,1152]{1,0:T(8,128)}, f32[8,1152]{1,0:T(8,128)}) fusion(f32[16,1152]{1,0:T(8,128)S(1)} %shard_map.77), kind=kLoop, calls=%fused_computation | loop fusion | bytes 147456 | tf_op jit(solution)/shard_map/slice | solution.py:263

commit v3 on v2

--- a/solution.py
+++ b/solution.py
@@ -12,6 +12,10 @@
 LANES = 128
 F32 = jnp.float32
 BF16 = jnp.bfloat16
+GRP_STEPS = (11, 15, 7, 10, 14, 6, 9, 13, 5, 8, 12, 4, 3, 2, 1)
+Z_STEPS = (4, 3, 5, 2, 6, 1, 7)
+KEYS, VALUES, TEXT_ONE, TEXT_PAIRS, MIXED, EMBED, IMAGE = 0, 1, 2, 3, 4, 5, 6
+PHASES = 7
 
 
 def dot_rows(left, right):
@@ -38,6 +42,22 @@
     column = lax.broadcasted_iota(jnp.int32, (rows, columns), 1)
     target = jnp.where(row == column, 1.0, 0.0)
     return (jax.nn.sigmoid(10.0 * logits - 2.0) - target).astype(BF16)
+
+
+def pack_block(block):
+    size = block.shape[1]
+    low, room = 2 * size // 3, LANES - size
+    rest = block[low:]
+    blank = jnp.zeros((size - low, 2 * room - size), F32)
+    over = jnp.concatenate([rest[:, room:], blank], axis=1)
+    right = jnp.concatenate([rest[:, :room], over], axis=0)
+    return jnp.concatenate([block[:low], right], axis=1)
+
+
+def unpack_block(packed, size):
+    half, room = size // 3, LANES - size
+    rest = jnp.concatenate([packed[:half, size:], packed[half:, size : 2 * size - room]], axis=1)
+    return jnp.concatenate([packed[:, :size], rest], axis=0)
 
 
 def kernel(
@@ -60,7 +80,6 @@
     key_all,
     value_send,
     value_all,
-    text_send,
     text_all,
     mixed_send,
     mixed_all,
@@ -77,6 +96,9 @@
     width = texts.shape[1]
     head_size = width // HEADS
     patch_count = patches.shape[0] // rows
+    n_z = n_blk // 2
+    z, x_hi = lax.rem(b, n_z), lax.div(b, n_z)
+    first_text = (z * 2 + x_hi) * rows
 
     loads = {}
     for index, (name, source, target) in enumerate(
@@ -93,41 +115,39 @@
         loads[name].start()
 
     def grp_peer(step):
-        return jnp.bitwise_xor(g, step)
-
-    def blk_peer(step):
-        return jnp.bitwise_xor(b, step)
+        return (jnp.bitwise_xor(g, step), b)
+
+    def blk_peer(turn, step):
+        return (g, lax.rem(x_hi + turn, 2) * n_z + lax.rem(z + step, n_z))
 
     barrier = pltpu.get_barrier_semaphore()
-    for step in range(1, n_grp):
-        pl.semaphore_signal(barrier, inc=1, device_id=(grp_peer(step), b), device_id_type=MESH)
-    for step in range(1, n_blk):
-        pl.semaphore_signal(barrier, inc=1, device_id=(g, blk_peer(step)), device_id_type=MESH)
-
-    def scatter(phase, source, target, axis, same):
-        count = n_grp if axis == "grp" else n_blk
-        for step in range(count - 1, 0, -1):
-            peer = grp_peer(step) if axis == "grp" else blk_peer(step)
-            device = (peer, b) if axis == "grp" else (g, peer)
-            pltpu.make_async_remote_copy(
-                src_ref=source if same else source.at[peer],
-                dst_ref=target.at[g if axis == "grp" else b],
-                send_sem=send_sem.at[phase],
-                recv_sem=recv_sem.at[phase],
-                device_id=device,
-                device_id_type=MESH,
-            ).start()
-
-    def total_of(phase, target):
-        many = target.at[pl.ds(0, target.shape[0] - 1)]
+    for step in GRP_STEPS:
+        pl.semaphore_signal(barrier, inc=1, device_id=grp_peer(step), device_id_type=MESH)
+    blk_peers = [blk_peer(1, step) for step in Z_STEPS + (0,)] + [blk_peer(0, step) for step in Z_STEPS]
+    for peer in blk_peers:
+        pl.semaphore_signal(barrier, inc=1, device_id=peer, device_id_type=MESH)
+
+    def copy(phase, source, target, device):
         return pltpu.make_async_remote_copy(
-            src_ref=many,
-            dst_ref=many,
+            src_ref=source,
+            dst_ref=target,
             send_sem=send_sem.at[phase],
             recv_sem=recv_sem.at[phase],
-            device_id=(g, b),
+            device_id=device,
             device_id_type=MESH,
         )
+
+    def total_of(phase):
+        many = {
+            KEYS: key_all.at[pl.ds(0, n_grp - 1)],
+            VALUES: value_all.at[pl.ds(0, n_grp - 1)],
+            TEXT_ONE: text_all.at[0, 0],
+            TEXT_PAIRS: text_all.at[pl.ds(0, n_z - 1)],
+            MIXED: mixed_all.at[pl.ds(0, n_grp - 1)],
+            EMBED: embed_all.at[pl.ds(0, n_grp - 1)],
+            IMAGE: image_all.at[pl.ds(0, n_blk - 1)],
+        }[phase]
+        return copy(phase, many, many, (g, b))
 
     column = lax.broadcasted_iota(jnp.int32, (HEADS, width), 1)
     head = lax.broadcasted_iota(jnp.int32, (HEADS, width), 0)
@@ -143,25 +163,25 @@
 
     loads["text"].wait()
     unit_text, inverse_text = unit_rows(texts[...].astype(F32))
-    text_send[...] = unit_text.astype(BF16)
-    text_all[pl.ds(b, 1)] = text_send[...][None]
+    unit_text_b = unit_text.astype(BF16)
+    text_all[pl.ds(z, 1), pl.ds(x_hi, 1)] = unit_text_b[None, None]
+
+    pl.semaphore_wait(barrier, n_grp + n_blk - 2)
+    for step in GRP_STEPS:
+        copy(KEYS, key_send, key_all.at[g], grp_peer(step)).start()
+    copy(TEXT_ONE, text_all.at[z, x_hi], text_all.at[z, x_hi], blk_peer(1, 0)).start()
 
     loads["value"].wait()
     value_f = w_value[...].astype(F32)
-    value_send[...] = jnp.zeros(value_send.shape, BF16)
     for h in range(HEADS):
-        piece = value_f[:, h * head_size : (h + 1) * head_size]
-        value_send[h, :head_size, :head_size] = piece.astype(BF16)
+        value_send[h] = pack_block(value_f[:, h * head_size : (h + 1) * head_size]).astype(BF16)
     value_all[pl.ds(g, 1)] = value_send[pl.ds(g, 1)]
-
-    pl.semaphore_wait(barrier, n_grp + n_blk - 2)
-
-    scatter(0, key_send, key_all, "grp", True)
-    scatter(1, value_send, value_all, "grp", False)
-    scatter(2, text_send, text_all, "blk", True)
+    for step in GRP_STEPS:
+        peer = grp_peer(step)
+        copy(VALUES, value_send.at[peer[0]], value_all.at[g], peer).start()
 
     loads["patches"].wait()
-    total_of(0, key_all).wait_recv()
+    total_of(KEYS).wait_recv()
     probe_keys = jnp.concatenate([key_all[i][:, :head_size] for i in range(n_grp)], axis=1)
     top_part = probe_keys.astype(BF16)
     rest = probe_keys - top_part.astype(F32)
@@ -183,39 +203,49 @@
     mixed = dot(expo, patches[...]) / denominator
     mixed_send[...] = mixed.reshape(HEADS, rows, width).astype(BF16)
     mixed_all[pl.ds(g, 1)] = mixed_send[pl.ds(g, 1)]
-    scatter(3, mixed_send, mixed_all, "grp", False)
-
-    total_of(1, value_all).wait_recv()
-    value_head = value_all[...][:, :head_size, :].astype(F32).reshape(width, LANES).astype(BF16)
+    for step in GRP_STEPS:
+        peer = grp_peer(step)
+        copy(MIXED, mixed_send.at[peer[0]], mixed_all.at[g], peer).start()
+
+    total_of(TEXT_ONE).wait_recv()
+    for step in Z_STEPS:
+        copy(TEXT_PAIRS, text_all.at[z], text_all.at[z], blk_peer(0, step)).start()
+
+    total_of(VALUES).wait_recv()
+    value_head = jnp.concatenate(
+        [unpack_block(value_all[i].astype(F32), head_size) for i in range(n_grp)], axis=0
+    ).astype(BF16)
     loads["out"].wait()
-    total_of(3, mixed_all).wait_recv()
+    total_of(MIXED).wait_recv()
     mixed_head = mixed_all[...].astype(F32).reshape(n_grp * rows, width).astype(BF16)
-    pooled = dot(mixed_head, value_head)[:, :head_size].astype(BF16)
+    pooled = dot(mixed_head, value_head).astype(BF16)
     partial_embed = dot(pooled, w_out[...])
     embed_send[...] = partial_embed.reshape(n_grp, rows, width).astype(BF16)
     embed_all[pl.ds(g, 1)] = embed_send[pl.ds(g, 1)]
-    scatter(4, embed_send, embed_all, "grp", False)
-
-    total_of(2, text_all).wait_recv()
+    for step in GRP_STEPS:
+        peer = grp_peer(step)
+        copy(EMBED, embed_send.at[peer[0]], embed_all.at[g], peer).start()
+
+    total_of(TEXT_PAIRS).wait_recv()
     all_texts = text_all[...].astype(F32).reshape(n_blk * rows, width).astype(BF16)
-    total_of(4, embed_all).wait_recv()
-    embed = jnp.sum(embed_all[...].astype(F32), axis=0)
-    unit_image, inverse_image = unit_rows(embed)
+    total_of(EMBED).wait_recv()
+    unit_image, inverse_image = unit_rows(jnp.sum(embed_all[...].astype(F32), axis=0))
     unit_image_b = unit_image.astype(BF16)
     image_send[...] = unit_image_b
     image_all[pl.ds(b, 1)] = unit_image_b[None]
-    scatter(5, image_send, image_all, "blk", True)
-
-    slopes = slopes_of(dot_rows(unit_image_b, all_texts), b * rows)
+    for peer in [(g, jnp.bitwise_xor(b, k)) for k in range(15, 0, -1)]:
+        copy(IMAGE, image_send, image_all.at[b], peer).start()
+
+    slopes = slopes_of(dot_rows(unit_image_b, all_texts), first_text)
     grads_ref[:rows] = chain_back(10.0 * dot(slopes, all_texts), unit_image, inverse_image)
 
-    total_of(5, image_all).wait_recv()
+    total_of(IMAGE).wait_recv()
     all_images = image_all[...].astype(F32).reshape(n_blk * rows, width).astype(BF16)
-    slopes = slopes_of(dot_rows(text_send[...], all_images), b * rows)
+    slopes = slopes_of(dot_rows(unit_text_b, all_images), b * rows)
     grads_ref[rows:] = chain_back(10.0 * dot(slopes, all_images), unit_text, inverse_text)
 
-    for phase, target in enumerate((key_all, value_all, text_all, mixed_all, embed_all, image_all)):
-        total_of(phase, target).wait_send()
+    for phase in range(PHASES):
+        total_of(phase).wait_send()
 
 
 def solution(mesh):
@@ -224,7 +254,7 @@
     def local(patches, probe, w_key, w_value, w_out, texts):
         rows, patch_count, width = patches.shape
         depth = w_key.shape[0]
-        padded = -(-depth // 16) * 16
+        packed = 2 * depth // 3
         hbm = pl.BlockSpec(memory_space=pltpu.HBM)
         vmem = pl.BlockSpec(memory_space=pltpu.VMEM)
         operands = (patches.reshape(rows * patch_count, width), probe, w_key, w_value, w_out, texts)
@@ -242,10 +272,9 @@
                 pltpu.VMEM((rows, width), BF16),
                 pltpu.VMEM((HEADS, LANES), F32),
                 pltpu.VMEM((n_grp, HEADS, LANES), F32),
-                pltpu.VMEM((n_grp, padded, LANES), BF16),
-                pltpu.VMEM((n_grp, padded, LANES), BF16),
-                pltpu.VMEM((rows, width), BF16),
-                pltpu.VMEM((n_blk, rows, width), BF16),
+                pltpu.VMEM((n_grp, packed, LANES), BF16),
+                pltpu.VMEM((n_grp, packed, LANES), BF16),
+                pltpu.VMEM((n_blk // 2, 2, rows, width), BF16),
                 pltpu.VMEM((n_grp, rows, width), BF16),
                 pltpu.VMEM((n_grp, rows, width), BF16),
                 pltpu.VMEM((n_grp, rows, width), BF16),
@@ -253,8 +282,8 @@
                 pltpu.VMEM((rows, width), BF16),
                 pltpu.VMEM((n_blk, rows, width), BF16),
                 pltpu.SemaphoreType.DMA((6,)),
-                pltpu.SemaphoreType.DMA((6,)),
-                pltpu.SemaphoreType.DMA((6,)),
+                pltpu.SemaphoreType.DMA((PHASES,)),
+                pltpu.SemaphoreType.DMA((PHASES,)),
             ],
             compiler_params=pltpu.CompilerParams(
                 collective_id=0, has_side_effects=True, vmem_limit_bytes=24 << 20

time: 40.3 us -> 37.6 us (0.933)
  the two profiles are of different devices: /device:TPU:2 before, /device:TPU:1 now
where the time goes in v3:
time: 37.6 us; the launch traced here: 37.5 us
  Pallas kernels  36.2 us (96%)
  between operations  0.64 us (2%)
  local copies, waits for them, and re-layouts  0.63 us (2%)
    pallas_call x1, Pallas kernels, local(): pl.pallas_call(lambda *refs: kernel(n_grp, n_blk, *refs), out_shape=pltpu...  36.2 us

profile of v3, /device:TPU:1, one launch (start us, length us, event | category | flops | bytes accessed | tf_op | source)
XLA Modules:
  0.0 37.5 jit_solution(8823718862979617449)
XLA Ops:
  0.6 36.2 %shard_map.77 = f32[16,1152]{1,0:T(8,128)S(1)} custom-call(bf16[512,1152]{1,0:T(8,128)(2,1)} %bitcast.1, bf16[1152]{0:T(1024)(128)(2,1)} %refs_1_.1, bf16[72,1152]{1,0:T(8,128)(2,1)} %refs_2_.1, bf16[72,1152]{1,0:T(8,128)(2,1)} %refs_3_.1, bf16[72,1152]{1,0:T(8,128)(2,1)} %refs_4_.1, bf16[8,1152]{1,0:T(8,128)(2,1)} %refs_5_.1), custom_call_target="tpu_custom_call" | custom-call | tf_op jit(solution)/shard_map/pallas_call | solution.py:261
  36.9 0.6 %fusion = (f32[8,1152]{1,0:T(8,128)}, f32[8,1152]{1,0:T(8,128)}) fusion(f32[16,1152]{1,0:T(8,128)S(1)} %shard_map.77), kind=kLoop, calls=%fused_computation | loop fusion | bytes 147456 | tf_op jit(solution)/shard_map/slice | solution.py:292

commit v4 on v3

--- a/solution.py
+++ b/solution.py
@@ -14,6 +14,8 @@
 BF16 = jnp.bfloat16
 GRP_STEPS = (11, 15, 7, 10, 14, 6, 9, 13, 5, 8, 12, 4, 3, 2, 1)
 Z_STEPS = (4, 3, 5, 2, 6, 1, 7)
+BLK_ORDER = (0, 1, 2, 8, 3, 9, 10, 11, 4, 7, 5, 6, 12, 15, 13, 14)
+BLK_ORDER_ODD = (0, 8, 1, 9, 2, 10, 3, 11, 4, 7, 5, 6, 12, 15, 13, 14)
 KEYS, VALUES, TEXT_ONE, TEXT_PAIRS, MIXED, EMBED, IMAGE = 0, 1, 2, 3, 4, 5, 6
 PHASES = 7
 
@@ -100,6 +102,19 @@
     z, x_hi = lax.rem(b, n_z), lax.div(b, n_z)
     first_text = (z * 2 + x_hi) * rows
 
+    def grp_peer(step):
+        return (jnp.bitwise_xor(g, step), b)
+
+    def blk_peer(turn, step):
+        return (g, lax.rem(x_hi + turn, 2) * n_z + lax.rem(z + step, n_z))
+
+    barrier = pltpu.get_barrier_semaphore()
+    for step in GRP_STEPS:
+        pl.semaphore_signal(barrier, inc=1, device_id=grp_peer(step), device_id_type=MESH)
+    blk_peers = [blk_peer(1, step) for step in Z_STEPS + (0,)] + [blk_peer(0, step) for step in Z_STEPS]
+    for peer in blk_peers:
+        pl.semaphore_signal(barrier, inc=1, device_id=peer, device_id_type=MESH)
+
     loads = {}
     for index, (name, source, target) in enumerate(
         (
@@ -114,19 +129,6 @@
         loads[name] = pltpu.make_async_copy(source, target, load_sem.at[index])
         loads[name].start()
 
-    def grp_peer(step):
-        return (jnp.bitwise_xor(g, step), b)
-
-    def blk_peer(turn, step):
-        return (g, lax.rem(x_hi + turn, 2) * n_z + lax.rem(z + step, n_z))
-
-    barrier = pltpu.get_barrier_semaphore()
-    for step in GRP_STEPS:
-        pl.semaphore_signal(barrier, inc=1, device_id=grp_peer(step), device_id_type=MESH)
-    blk_peers = [blk_peer(1, step) for step in Z_STEPS + (0,)] + [blk_peer(0, step) for step in Z_STEPS]
-    for peer in blk_peers:
-        pl.semaphore_signal(barrier, inc=1, device_id=peer, device_id_type=MESH)
-
     def copy(phase, source, target, device):
         return pltpu.make_async_remote_copy(
             src_ref=source,
@@ -182,6 +184,9 @@
 
     loads["patches"].wait()
     total_of(KEYS).wait_recv()
+    total_of(TEXT_ONE).wait_recv()
+    for step in Z_STEPS:
+        copy(TEXT_PAIRS, text_all.at[z], text_all.at[z], blk_peer(0, step)).start()
     probe_keys = jnp.concatenate([key_all[i][:, :head_size] for i in range(n_grp)], axis=1)
     top_part = probe_keys.astype(BF16)
     rest = probe_keys - top_part.astype(F32)
@@ -207,9 +212,6 @@
         peer = grp_peer(step)
         copy(MIXED, mixed_send.at[peer[0]], mixed_all.at[g], peer).start()
 
-    total_of(TEXT_ONE).wait_recv()
-    for step in Z_STEPS:
-        copy(TEXT_PAIRS, text_all.at[z], text_all.at[z], blk_peer(0, step)).start()
 
     total_of(VALUES).wait_recv()
     value_head = jnp.concatenate(
@@ -217,7 +219,7 @@
     ).astype(BF16)
     loads["out"].wait()
     total_of(MIXED).wait_recv()
-    mixed_head = mixed_all[...].astype(F32).reshape(n_grp * rows, width).astype(BF16)
+    mixed_head = mixed_all[...].reshape(n_grp * rows, width)
     pooled = dot(mixed_head, value_head).astype(BF16)
     partial_embed = dot(pooled, w_out[...])
     embed_send[...] = partial_embed.reshape(n_grp, rows, width).astype(BF16)
@@ -226,21 +228,27 @@
         peer = grp_peer(step)
         copy(EMBED, embed_send.at[peer[0]], embed_all.at[g], peer).start()
 
-    total_of(TEXT_PAIRS).wait_recv()
-    all_texts = text_all[...].astype(F32).reshape(n_blk * rows, width).astype(BF16)
     total_of(EMBED).wait_recv()
     unit_image, inverse_image = unit_rows(jnp.sum(embed_all[...].astype(F32), axis=0))
     unit_image_b = unit_image.astype(BF16)
     image_send[...] = unit_image_b
     image_all[pl.ds(b, 1)] = unit_image_b[None]
-    for peer in [(g, jnp.bitwise_xor(b, k)) for k in range(15, 0, -1)]:
-        copy(IMAGE, image_send, image_all.at[b], peer).start()
+    odd = lax.rem(lax.div(g, 2), 2)
+    for even_target, odd_target in zip(BLK_ORDER, BLK_ORDER_ODD, strict=True):
+        target = jnp.where(odd == 0, even_target, odd_target)
+
+        @pl.when(b != target)
+        def send_image(target=target):
+            copy(IMAGE, image_send, image_all.at[b], (g, target)).start()
+
+    total_of(TEXT_PAIRS).wait_recv()
+    all_texts = text_all[...].reshape(n_blk * rows, width)
 
     slopes = slopes_of(dot_rows(unit_image_b, all_texts), first_text)
     grads_ref[:rows] = chain_back(10.0 * dot(slopes, all_texts), unit_image, inverse_image)
 
     total_of(IMAGE).wait_recv()
-    all_images = image_all[...].astype(F32).reshape(n_blk * rows, width).astype(BF16)
+    all_images = image_all[...].reshape(n_blk * rows, width)
     slopes = slopes_of(dot_rows(unit_text_b, all_images), b * rows)
     grads_ref[rows:] = chain_back(10.0 * dot(slopes, all_images), unit_text, inverse_text)
 

time: 37.6 us -> 36.4 us (0.968)
  the two profiles are of different devices: /device:TPU:1 before, /device:TPU:4 now
where the time goes in v4:
time: 36.4 us; the launch traced here: 36.1 us
  Pallas kernels  34.9 us (96%)
  between operations  0.64 us (2%)
  local copies, waits for them, and re-layouts  0.63 us (2%)
    pallas_call x1, Pallas kernels, local(): pl.pallas_call(lambda *refs: kernel(n_grp, n_blk, *refs), out_shape=pltpu...  34.9 us

profile of v4, /device:TPU:4, one launch (start us, length us, event | category | flops | bytes accessed | tf_op | source)
XLA Modules:
  0.0 36.1 jit_solution(9032362321080690761)
XLA Ops:
  0.6 34.9 %shard_map.77 = f32[16,1152]{1,0:T(8,128)S(1)} custom-call(bf16[512,1152]{1,0:T(8,128)(2,1)} %bitcast.1, bf16[1152]{0:T(1024)(128)(2,1)} %refs_1_.1, bf16[72,1152]{1,0:T(8,128)(2,1)} %refs_2_.1, bf16[72,1152]{1,0:T(8,128)(2,1)} %refs_3_.1, bf16[72,1152]{1,0:T(8,128)(2,1)} %refs_4_.1, bf16[8,1152]{1,0:T(8,128)(2,1)} %refs_5_.1), custom_call_target="tpu_custom_call" | custom-call | tf_op jit(solution)/shard_map/pallas_call | solution.py:269
  35.5 0.6 %fusion = (f32[8,1152]{1,0:T(8,128)}, f32[8,1152]{1,0:T(8,128)}) fusion(f32[16,1152]{1,0:T(8,128)S(1)} %shard_map.77), kind=kLoop, calls=%fused_computation | loop fusion | bytes 147456 | tf_op jit(solution)/shard_map/slice | solution.py:300

commit v5 on v4

--- a/solution.py
+++ b/solution.py
@@ -14,8 +14,8 @@
 BF16 = jnp.bfloat16
 GRP_STEPS = (11, 15, 7, 10, 14, 6, 9, 13, 5, 8, 12, 4, 3, 2, 1)
 Z_STEPS = (4, 3, 5, 2, 6, 1, 7)
-BLK_ORDER = (0, 1, 2, 8, 3, 9, 10, 11, 4, 7, 5, 6, 12, 15, 13, 14)
-BLK_ORDER_ODD = (0, 8, 1, 9, 2, 10, 3, 11, 4, 7, 5, 6, 12, 15, 13, 14)
+BLK_ORDER = (0, 8, 1, 9, 2, 10, 3, 11, 4, 7, 5, 6, 12, 15, 13, 14)
+BLK_ORDER_HIGH = (0, 1, 2, 8, 9, 10, 3, 11, 4, 7, 5, 6, 12, 15, 13, 14)
 KEYS, VALUES, TEXT_ONE, TEXT_PAIRS, MIXED, EMBED, IMAGE = 0, 1, 2, 3, 4, 5, 6
 PHASES = 7
 
@@ -178,7 +178,7 @@
     for h in range(HEADS):
         value_send[h] = pack_block(value_f[:, h * head_size : (h + 1) * head_size]).astype(BF16)
     value_all[pl.ds(g, 1)] = value_send[pl.ds(g, 1)]
-    for step in GRP_STEPS:
+    for step in GRP_STEPS[::-1]:
         peer = grp_peer(step)
         copy(VALUES, value_send.at[peer[0]], value_all.at[g], peer).start()
 
@@ -205,7 +205,7 @@
     spread = jnp.where(inside, spread, -jnp.inf)
     expo = jnp.exp(spread - jnp.max(spread, axis=1, keepdims=True)).astype(BF16)
     denominator = jnp.sum(expo.astype(F32), axis=1, keepdims=True)
-    mixed = dot(expo, patches[...]) / denominator
+    mixed = dot(expo, patches[...]) * (1.0 / denominator)
     mixed_send[...] = mixed.reshape(HEADS, rows, width).astype(BF16)
     mixed_all[pl.ds(g, 1)] = mixed_send[pl.ds(g, 1)]
     for step in GRP_STEPS:
@@ -233,9 +233,8 @@
     unit_image_b = unit_image.astype(BF16)
     image_send[...] = unit_image_b
     image_all[pl.ds(b, 1)] = unit_image_b[None]
-    odd = lax.rem(lax.div(g, 2), 2)
-    for even_target, odd_target in zip(BLK_ORDER, BLK_ORDER_ODD, strict=True):
-        target = jnp.where(odd == 0, even_target, odd_target)
+    for low_target, high_target in zip(BLK_ORDER, BLK_ORDER_HIGH, strict=True):
+        target = jnp.where(x_hi == 0, low_target, high_target)
 
         @pl.when(b != target)
         def send_image(target=target):

time: 36.4 us -> 36.2 us (level)
  no operation moved by 1% of the time
where the time goes in v5:
time: 36.2 us; the launch traced here: 35.8 us
  Pallas kernels  34.6 us (96%)
  between operations  0.64 us (2%)
  local copies, waits for them, and re-layouts  0.63 us (2%)
    pallas_call x1, Pallas kernels, local(): pl.pallas_call(lambda *refs: kernel(n_grp, n_blk, *refs), out_shape=pltpu...  34.6 us

profile of v5, /device:TPU:4, one launch (start us, length us, event | category | flops | bytes accessed | tf_op | source)
XLA Modules:
  0.0 35.8 jit_solution(10374410952247238355)
XLA Ops:
  0.6 34.6 %shard_map.77 = f32[16,1152]{1,0:T(8,128)S(1)} custom-call(bf16[512,1152]{1,0:T(8,128)(2,1)} %bitcast.1, bf16[1152]{0:T(1024)(128)(2,1)} %refs_1_.1, bf16[72,1152]{1,0:T(8,128)(2,1)} %refs_2_.1, bf16[72,1152]{1,0:T(8,128)(2,1)} %refs_3_.1, bf16[72,1152]{1,0:T(8,128)(2,1)} %refs_4_.1, bf16[8,1152]{1,0:T(8,128)(2,1)} %refs_5_.1), custom_call_target="tpu_custom_call" | custom-call | tf_op jit(solution)/shard_map/pallas_call | solution.py:268
  35.2 0.6 %fusion = (f32[8,1152]{1,0:T(8,128)}, f32[8,1152]{1,0:T(8,128)}) fusion(f32[16,1152]{1,0:T(8,128)S(1)} %shard_map.77), kind=kLoop, calls=%fused_computation | loop fusion | bytes 147456 | tf_op jit(solution)/shard_map/slice | solution.py:299

commit v6 on v5

--- a/solution.py
+++ b/solution.py
@@ -184,9 +184,6 @@
 
     loads["patches"].wait()
     total_of(KEYS).wait_recv()
-    total_of(TEXT_ONE).wait_recv()
-    for step in Z_STEPS:
-        copy(TEXT_PAIRS, text_all.at[z], text_all.at[z], blk_peer(0, step)).start()
     probe_keys = jnp.concatenate([key_all[i][:, :head_size] for i in range(n_grp)], axis=1)
     top_part = probe_keys.astype(BF16)
     rest = probe_keys - top_part.astype(F32)
@@ -214,6 +211,9 @@
 
 
     total_of(VALUES).wait_recv()
+    total_of(TEXT_ONE).wait_recv()
+    for step in Z_STEPS:
+        copy(TEXT_PAIRS, text_all.at[z], text_all.at[z], blk_peer(0, step)).start()
     value_head = jnp.concatenate(
         [unpack_block(value_all[i].astype(F32), head_size) for i in range(n_grp)], axis=0
     ).astype(BF16)

time: 36.2 us -> 36.3 us (level)
  no operation moved by 1% of the time
where the time goes in v6:
time: 36.3 us; the launch traced here: 35.7 us
  Pallas kernels  34.5 us (95%)
  between operations  0.64 us (2%)
  local copies, waits for them, and re-layouts  0.63 us (2%)
    pallas_call x1, Pallas kernels, local(): pl.pallas_call(lambda *refs: kernel(n_grp, n_blk, *refs), out_shape=pltpu...  34.5 us

profile of v6, /device:TPU:4, one launch (start us, length us, event | category | flops | bytes accessed | tf_op | source)
XLA Modules:
  0.0 35.7 jit_solution(14300526702724212440)
XLA Ops:
  0.6 34.5 %shard_map.77 = f32[16,1152]{1,0:T(8,128)S(1)} custom-call(bf16[512,1152]{1,0:T(8,128)(2,1)} %bitcast.1, bf16[1152]{0:T(1024)(128)(2,1)} %refs_1_.1, bf16[72,1152]{1,0:T(8,128)(2,1)} %refs_2_.1, bf16[72,1152]{1,0:T(8,128)(2,1)} %refs_3_.1, bf16[72,1152]{1,0:T(8,128)(2,1)} %refs_4_.1, bf16[8,1152]{1,0:T(8,128)(2,1)} %refs_5_.1), custom_call_target="tpu_custom_call" | custom-call | tf_op jit(solution)/shard_map/pallas_call | solution.py:268
  35.1 0.6 %fusion = (f32[8,1152]{1,0:T(8,128)}, f32[8,1152]{1,0:T(8,128)}) fusion(f32[16,1152]{1,0:T(8,128)S(1)} %shard_map.77), kind=kLoop, calls=%fused_computation | loop fusion | bytes 147456 | tf_op jit(solution)/shard_map/slice | solution.py:299

commit v7 on v6

--- a/solution.py
+++ b/solution.py
@@ -229,10 +229,9 @@
         copy(EMBED, embed_send.at[peer[0]], embed_all.at[g], peer).start()
 
     total_of(EMBED).wait_recv()
-    unit_image, inverse_image = unit_rows(jnp.sum(embed_all[...].astype(F32), axis=0))
-    unit_image_b = unit_image.astype(BF16)
-    image_send[...] = unit_image_b
-    image_all[pl.ds(b, 1)] = unit_image_b[None]
+    embed = jnp.sum(embed_all[...].astype(F32), axis=0)
+    image_send[...] = embed.astype(BF16)
+    image_all[pl.ds(b, 1)] = image_send[...][None]
     for low_target, high_target in zip(BLK_ORDER, BLK_ORDER_HIGH, strict=True):
         target = jnp.where(x_hi == 0, low_target, high_target)
 
@@ -240,6 +239,8 @@
         def send_image(target=target):
             copy(IMAGE, image_send, image_all.at[b], (g, target)).start()
 
+    unit_image, inverse_image = unit_rows(embed)
+    unit_image_b = unit_image.astype(BF16)
     total_of(TEXT_PAIRS).wait_recv()
     all_texts = text_all[...].reshape(n_blk * rows, width)
 
@@ -247,7 +248,8 @@
     grads_ref[:rows] = chain_back(10.0 * dot(slopes, all_texts), unit_image, inverse_image)
 
     total_of(IMAGE).wait_recv()
-    all_images = image_all[...].reshape(n_blk * rows, width)
+    all_images = image_all[...].astype(F32).reshape(n_blk * rows, width)
+    all_images = unit_rows(all_images)[0].astype(BF16)
     slopes = slopes_of(dot_rows(unit_text_b, all_images), b * rows)
     grads_ref[rows:] = chain_back(10.0 * dot(slopes, all_images), unit_text, inverse_text)
 

time: 36.3 us -> 36.3 us (level)
  no operation moved by 1% of the time
where the time goes in v7:
time: 36.3 us; the launch traced here: 35.8 us
  Pallas kernels  34.5 us (95%)
  between operations  0.64 us (2%)
  local copies, waits for them, and re-layouts  0.63 us (2%)
    pallas_call x1, Pallas kernels, local(): pl.pallas_call(lambda *refs: kernel(n_grp, n_blk, *refs), out_shape=pltpu...  34.5 us

profile of v7, /device:TPU:4, one launch (start us, length us, event | category | flops | bytes accessed | tf_op | source)
XLA Modules:
  0.0 35.8 jit_solution(10081084310742751087)
XLA Ops:
  0.6 34.5 %shard_map.77 = f32[16,1152]{1,0:T(8,128)S(1)} custom-call(bf16[512,1152]{1,0:T(8,128)(2,1)} %bitcast.1, bf16[1152]{0:T(1024)(128)(2,1)} %refs_1_.1, bf16[72,1152]{1,0:T(8,128)(2,1)} %refs_2_.1, bf16[72,1152]{1,0:T(8,128)(2,1)} %refs_3_.1, bf16[72,1152]{1,0:T(8,128)(2,1)} %refs_4_.1, bf16[8,1152]{1,0:T(8,128)(2,1)} %refs_5_.1), custom_call_target="tpu_custom_call" | custom-call | tf_op jit(solution)/shard_map/pallas_call | solution.py:270
  35.1 0.6 %fusion = (f32[8,1152]{1,0:T(8,128)}, f32[8,1152]{1,0:T(8,128)}) fusion(f32[16,1152]{1,0:T(8,128)S(1)} %shard_map.77), kind=kLoop, calls=%fused_computation | loop fusion | bytes 147456 | tf_op jit(solution)/shard_map/slice | solution.py:301
